TPU v7x, 512 devices: a whole 4x8x8 slice. The times are simulated.
512 devices in a mesh: dp: 8 (over y), feat: 64 (over x, z, core).
Axes of the slice: x: 4, y: 8, z: 8, core: 2. Of those that a mesh axis runs over, the one named last changes fastest.
Arguments:
- features: bfloat16 [8, 16384, 128], P('dp', None, 'feat'), may hold values from -6 to 6
- tile_weights: bfloat16 [8, 1536, 128, 128], P('dp', 'feat'), may hold values from -0.15625 to 0.15625
- tile_rows: int32 [8, 1536], P('dp', 'feat'), may hold values from 0 to 1
- tile_owners: int32 [8, 1536, 1], P('dp', 'feat'), may hold values from 0 to 63; in each aligned block of 24 rows (0 to 23, 24 to 47, ..., all dimensions but the last counted through in order) at most 2 rows name the same one
- tile_blocks: int32 [8, 1536], P('dp', 'feat'), may hold values from 0 to 1
- tile_counts: int32 [8, 64], P('dp', 'feat'), may hold values from 6 to 24, as said below
- cotangent: bfloat16 [8, 16384, 1024], P('dp', 'feat'), may hold values from -0.046875 to 0.046875
- w_self: bfloat16 [128, 1024], replicated, may hold values from -0.5 to 0.5
- w_neigh: bfloat16 [128, 1024], replicated, may hold values from -0.5 to 0.5
- bias: float32 [1024], replicated, may hold values from -4 to 4
Outputs:
- grad_self: float32 [128, 1024], P(None, 'feat')
- grad_neigh: float32 [128, 1024], P(None, 'feat')
- grad_bias: float32 [1024], P('feat')
Inputs may be any that keep to these rules, and one draw needn't show every extreme that they name: `tile_owners`: among the 24 tile slots of one device at most 2 name one owner, a bound that some block of them reaches. `tile_counts`: in every batch some device has all 24 slots live.
All inputs are finite; a program needn't handle non-finite values.
Results may differ from a plain program's by a relative error of at most 0.008.
Values may be sent and summed in bfloat16 or wider, within the bound.
No kernel may reach another device: no remote copies, remote signals or barrier semaphores. Data moves between devices by JAX's collectives and lax.ppermute only.
A program may use at most 64 MiB of HBM per device.

v0:
```python
import jax
import jax.numpy as jnp
from jax import lax
from jax.sharding import PartitionSpec as P


def silu_slope(pre_act):
    sigmoid_z = jax.nn.sigmoid(pre_act)
    return sigmoid_z * (1.0 + pre_act * (1.0 - sigmoid_z))


def local(
    features,
    tile_weights,
    tile_rows,
    tile_owners,
    tile_blocks,
    tile_counts,
    cotangent,
    w_self,
    w_neigh,
    bias,
):
    owned = lax.all_to_all(features, "feat", split_axis=1, concat_axis=2, tiled=True)[0]
    node_rows, feat_width = owned.shape
    slot_count = tile_weights.shape[1]
    tile_side = tile_weights.shape[2]
    row_blocks = node_rows // tile_side
    peer_count = lax.axis_size("feat")
    row_index = tile_rows[0]
    owner_index = tile_owners[0, :, 0]
    block_index = tile_blocks[0]
    live = jnp.arange(slot_count, dtype=jnp.int32) < tile_counts[0, 0]
    whole = lax.all_gather(owned, "feat", axis=0, tiled=True)
    picked = whole.reshape(-1, tile_side, feat_width)[owner_index * row_blocks + block_index]
    products = jnp.einsum(
        "kij,kjf->kif", tile_weights[0], picked, preferred_element_type=jnp.float32
    )
    select = (
        (row_index[None, :] == jnp.arange(row_blocks, dtype=jnp.int32)[:, None]) & live[None, :]
    ).astype(jnp.float32)
    summed = jnp.einsum("rk,kif->rif", select, products, precision=lax.Precision.HIGHEST)
    neighbour = summed.reshape(node_rows, feat_width).astype(jnp.bfloat16)
    pre_act = (
        jnp.dot(owned, w_self, preferred_element_type=jnp.float32)
        + jnp.dot(neighbour, w_neigh, preferred_element_type=jnp.float32)
        + bias
    )
    slope = (cotangent[0].astype(jnp.float32) * silu_slope(pre_act)).astype(jnp.bfloat16)
    grad_s = jnp.einsum("nf,nh->fh", owned, slope, preferred_element_type=jnp.float32)
    grad_n = jnp.einsum("nf,nh->fh", neighbour, slope, preferred_element_type=jnp.float32)
    grad_b = jnp.sum(slope.astype(jnp.float32), axis=0)
    total_s, total_n, total_b = lax.psum((grad_s, grad_n, grad_b), ("dp", "feat"))
    column_count = w_self.shape[1] // peer_count
    start = lax.axis_index("feat") * column_count
    out_s = lax.dynamic_slice_in_dim(total_s, start, column_count, 1)
    out_n = lax.dynamic_slice_in_dim(total_n, start, column_count, 1)
    out_b = lax.dynamic_slice_in_dim(total_b, start, column_count, 0)
    return (out_s, out_n, out_b)


def solution(mesh):
    return jax.shard_map(
        local,
        mesh=mesh,
        in_specs=(
            P("dp", None, "feat"),
            P("dp", "feat", None, None),
            P("dp", "feat"),
            P("dp", "feat", None),
            P("dp", "feat"),
            P("dp", "feat"),
            P("dp", "feat", None),
            P(),
            P(),
            P(),
        ),
        out_specs=(P(None, "feat"), P(None, "feat"), P("feat")),
        check_vma=False,
    )
```

profile of v0, /device:TPU:23, one launch (start us, length us, event | category | flops | bytes accessed | tf_op | source)
XLA Modules:
  0.0 554.2 jit_solution(6314317441695136422)
XLA Ops:
  7.2 15.4 %copy.26 = bf16[1,16384,2]{2,0,1:T(2,128)(2,1)} copy(bf16[1,16384,2]{1,2,0:T(2,128)(2,1)} %param.10) | data formatting | bytes 131072 | tf_op args[0]
  22.6 0.5 broadcast.52
  23.1 90.8 %reduce = bf16[16384,2]{1,0:T(8,128)(2,1)} reduce(bf16[16384,1,2]{2,1,0:T(2,128)(2,1)} %bitcast.51, bf16[]{:T(256)} %broadcast.52), dimensions={1}, to_apply=%bitcast.36.reduce_sub_computation | reduce | bytes 131074
  113.9 7.1 %reshape.61 = bf16[64,2,256]{2,1,0:T(2,128)(2,1)S(1)} reshape(bf16[16384,2]{1,0:T(8,128)(2,1)} %reduce) | data formatting | bytes 131072
  121.0 21.9 %all_to_all.15 = bf16[64,2,256]{2,1,0:T(2,128)(2,1)S(1)} all-to-all(bf16[64,2,256]{2,1,0:T(2,128)(2,1)S(1)} %reshape.61), channel_id=1, replica_groups=mesh['dp'=8,'feat'=64] {'feat'}, dimensions={0} | all-to-all | bytes 131072 | tf_op jit(solution)/shard_map/all_to_all | solution.py:24
  142.9 16.4 %reshape.62 = bf16[16384,1,2]{2,1,0:T(2,128)(2,1)} reshape(bf16[64,2,256]{2,1,0:T(2,128)(2,1)S(1)} %all_to_all.15) | data formatting | bytes 131072
  159.3 15.4 %copy.27 = bf16[1,16384,2]{1,2,0:T(2,128)(2,1)S(1)} copy(bf16[1,16384,2]{2,0,1:T(2,128)(2,1)} %bitcast.52) | data formatting | bytes 131072 | tf_op jit(solution)/shard_map/all_to_all | solution.py:24
  174.7 0.1 copy.28
  174.8 0.7 squeeze.14
  175.5 0.2 all-reduce.3.cloned.1.call-start
  176.4 1.2 fusion.10
  177.6 77.5 %all-gather.2.cloned.1.call-done = bf16[16384,128]{0,1:T(8,128)(2,1)} async-done(((bf16[256,128]{0,1:T(8,128)(2,1)}), bf16[16384,128]{0,1:T(8,128)(2,1)}) %all-gather.2.cloned.1.call-update) | async-done | bytes 4194320 | tf_op jit(solution)/shard_map/all_gather | solution.py:34
  255.0 6.4 %copy.29 = bf16[16384,128]{1,0:T(8,128)(2,1)} copy(bf16[16384,128]{0,1:T(8,128)(2,1)} %all-gather.2.cloned.1.call-done) | data formatting | bytes 8388608 | tf_op jit(solution)/shard_map/all_gather | solution.py:34
  261.4 2.9 gather_fusion
  264.4 1.9 convolution_bitcast_fusion
  266.2 2.0 copy.31
  268.2 0.6 convolution_convert_fusion
  268.9 1.8 convert_reduce_fusion
  270.6 1.1 fusion.11
  271.8 1.1 convolution_bitcast_fusion.1
  272.9 96.3 %psum.23 = f32[1024]{0:T(1024)S(1)} all-reduce(f32[1024]{0:T(1024)S(1)} %get-tuple-element.5), channel_id=1, replica_groups=mesh['dp'=8,'feat'=64] {'dp','feat'}, use_global_device_ids=true, to_apply=%region_3.0 | all-reduce | flops 1024 | bytes 8192 | tf_op jit(solution)/shard_map/psum | solution.py:53
  369.3 0.6 dynamic_slice.11
  369.9 176.2 %all-reduce.3.cloned.1.call-done = (f32[128,1024]{0,1:T(8,128)}, f32[128,1024]{0,1:T(8,128)}) async-done(((f32[128,1024]{0,1:T(8,128)}, f32[128,1024]{0,1:T(8,128)}), (f32[128,1024]{0,1:T(8,128)}, f32[128,1024]{0,1:T(8,128)})) %all-reduce.3.cloned.1.call-update) | async-done | bytes 1048592 | tf_op jit(solution)/shard_map/psum | solution.py:53
  546.0 1.3 constant_dynamic-slice_fusion
  (22 shorter events, 0.1 us)
Async XLA Ops:
  7.2 257.2 %copy-start = (bf16[1,24,128,128]{3,2,1,0:T(8,128)(2,1)S(1)}, bf16[1,24,128,128]{3,2,1,0:T(8,128)(2,1)}, u32[]{:S(2)}) copy-start(bf16[1,24,128,128]{3,2,1,0:T(8,128)(2,1)} %param.11) | copy-start | bytes 2359300
  7.2 247.8 %all-gather.2.cloned.1.call-start = ((), (), s32[]{:S(2)}) async-start(), calls=%async_computation.1 | async-start | bytes 4259840 | tf_op jit(solution)/shard_map/all_gather | solution.py:34
  159.3 17.1 %copy-start.5 = (s32[1,24]{1,0:T(1,128)S(1)}, s32[1,24]{1,0:T(1,128)}, u32[]{:S(2)}) copy-start(s32[1,24]{1,0:T(1,128)} %param.14) | copy-start | bytes 292
  159.3 17.1 %copy-start.6 = (s32[1,24,1]{1,2,0:T(1,128)S(1)}, s32[1,24,1]{1,2,0:T(1,128)}, u32[]{:S(2)}) copy-start(s32[1,24,1]{1,2,0:T(1,128)} %param.13) | copy-start | bytes 292
  159.3 17.1 %copy-start.2 = (bf16[128,1024]{1,0:T(8,128)(2,1)S(1)}, bf16[128,1024]{1,0:T(8,128)(2,1)}, u32[]{:S(2)}) copy-start(bf16[128,1024]{1,0:T(8,128)(2,1)} %param.17) | copy-start | bytes 786436
  175.5 370.6 %all-reduce.3.cloned.1.call-start = ((), (), s32[]{:S(2)}) async-start(), calls=%async_computation.2 | async-start | bytes 2097152 | tf_op jit(solution)/shard_map/psum | solution.py:53
  261.4 6.8 %copy-start.3 = (s32[1,24]{1,0:T(1,128)S(1)}, s32[1,24]{1,0:T(1,128)}, u32[]{:S(2)}) copy-start(s32[1,24]{1,0:T(1,128)} %param.12) | copy-start | bytes 292
  264.4 4.5 copy-start.4
  268.8 3.0 copy-start.1
Sparse Core Ops, SparseCore 0:
  175.6 79.3 all-gather.1
  273.1 272.9 all-reduce.2
where the time goes:
time: 556 us; the launch traced here: 554 us
  waiting for transfers between devices  254 us (46%)
  blocking collectives  118 us (21%)
  other arithmetic  90.8 us (16%)
  local copies, waits for them, and re-layouts  68.7 us (12%)
  between operations  14.9 us (3%)
  matrix products  7.67 us (1%)
    psum x1, waiting for transfers between devices, local(): lax.psum((grad_s, grad_n, grad_b), ('dp', 'feat'))  176 us
    psum x1, blocking collectives, local(): lax.psum((grad_s, grad_n, grad_b), ('dp', 'feat'))  96.3 us
    unnamed x1, other arithmetic  90.8 us
    all_gather x1, waiting for transfers between devices, local(): whole = lax.all_gather(owned, 'feat', axis=0, tiled=True)  77.5 us
    unnamed x19, local copies, waits for them, and re-layouts  39.5 us
    all_to_all x1, blocking collectives, local(): lax.all_to_all(features, 'feat', split_axis=1, concat_axis=2, tiled=True)[0]  21.9 us
    all_to_all x2, local copies, waits for them, and re-layouts, local(): lax.all_to_all(features, 'feat', split_axis=1, concat_axis=2, tiled=True)[0]  15.5 us
  transfers between devices with their start and end apart: 2, of which 2 were waited for; matrix products, arithmetic and copies ran while one was open for 0% of the time, Pallas kernels for 0%

commit v1 on v0

--- a/solution.py
+++ b/solution.py
@@ -2,6 +2,18 @@
 import jax.numpy as jnp
 from jax import lax
 from jax.sharding import PartitionSpec as P
+
+
+def trace_trees(dimension_no, shard_axis, out_dim, local_values):
+    return jnp.concatenate(
+        lax.all_to_all(
+            jnp.stack(jnp.split(local_values, lax.axis_size(shard_axis), axis=out_dim), axis=0),
+            shard_axis,
+            split_axis=0,
+            concat_axis=0,
+        ),
+        axis=dimension_no,
+    )
 
 
 def silu_slope(pre_act):
@@ -21,7 +33,7 @@
     w_neigh,
     bias,
 ):
-    owned = lax.all_to_all(features, "feat", split_axis=1, concat_axis=2, tiled=True)[0]
+    owned = trace_trees(2, "feat", 1, features)[0]
     node_rows, feat_width = owned.shape
     slot_count = tile_weights.shape[1]
     tile_side = tile_weights.shape[2]

time: 556 us -> 447 us (0.80)
  other arithmetic: 90.8 us -> 0.69 us
  local copies, waits for them, and re-layouts: 68.7 us -> 52 us
    unnamed x1 -> x0, other arithmetic: 90.8 us -> none
    all_to_all x2 -> x0, local copies, waits for them, and re-layouts: 15.5 us -> none  [local(): lax.all_to_all(features, 'feat', split_axis=1, concat_axis=2, tiled=True)[0]]
    all_gather x1 -> x0, local copies, waits for them, and re-layouts: 6.42 us -> none  [local(): whole = lax.all_gather(owned, 'feat', axis=0, tiled=True)]
    unnamed x19 -> x73, local copies, waits for them, and re-layouts: 39.5 us -> 43.8 us
  transfers between devices with their start and end apart: 2 -> 2, of which waited for: 2 -> 2; matrix products, arithmetic and copies ran while one was open for 0% -> 1% of each run, Pallas kernels for 0% -> 0%
where the time goes in v1:
time: 447 us; the launch traced here: 446 us
  waiting for transfers between devices  253 us (57%)
  blocking collectives  119 us (27%)
  local copies, waits for them, and re-layouts  52 us (12%)
  between operations  14.8 us (3%)
  matrix products  6.66 us (1%)
    psum x1, waiting for transfers between devices, local(): lax.psum((grad_s, grad_n, grad_b), ('dp', 'feat'))  175 us
    psum x1, blocking collectives, local(): lax.psum((grad_s, grad_n, grad_b), ('dp', 'feat'))  96.7 us
    all_gather x1, waiting for transfers between devices, local(): whole = lax.all_gather(owned, 'feat', axis=0, tiled=True)  78.2 us
    unnamed x73, local copies, waits for them, and re-layouts  43.8 us
    all_to_all x1, blocking collectives, trace_trees(): lax.all_to_all(jnp.stack(jnp.split(local_values, lax.axis_size(shard_axis...  21.9 us
  transfers between devices with their start and end apart: 2, of which 2 were waited for; matrix products, arithmetic and copies ran while one was open for 1% of the time, Pallas kernels for 0%

profile of v1, /device:TPU:23, one launch (start us, length us, event | category | flops | bytes accessed | tf_op | source)
XLA Modules:
  0.0 445.6 jit_solution(4177702184545146926)
XLA Ops:
  7.2 0.7 constant_dynamic-update-slice_fusion.63
  9.3 0.7 constant_dynamic-update-slice_fusion.60
  12.1 0.7 constant_dynamic-update-slice_fusion.56
  14.2 0.7 constant_dynamic-update-slice_fusion.53
  14.9 0.7 constant_dynamic-update-slice_fusion.52
  16.9 0.7 constant_dynamic-update-slice_fusion.49
  17.6 0.7 constant_dynamic-update-slice_fusion.48
  19.7 0.7 constant_dynamic-update-slice_fusion.45
  20.4 0.7 constant_dynamic-update-slice_fusion.44
  22.4 0.7 constant_dynamic-update-slice_fusion.41
  25.2 0.7 constant_dynamic-update-slice_fusion.37
  27.2 0.7 constant_dynamic-update-slice_fusion.34
  51.3 21.9 %all_to_all.5 = bf16[64,1,256,2]{2,3,1,0:T(2,128)(2,1)S(1)} all-to-all(bf16[64,1,256,2]{2,3,1,0:T(2,128)(2,1)S(1)} %constant_dynamic-update-slice_fusion), channel_id=1, replica_groups=mesh['dp'=8,'feat'=64] {'feat'}, dimensions={0} | all-to-all | bytes 131072 | tf_op jit(solution)/shard_map/all_to_all | solution.py:9
  73.2 0.7 copy.13
  75.4 1.3 fusion.16
  76.6 78.2 %all-gather.2.cloned.1.call-done = bf16[16384,128]{1,0:T(8,128)(2,1)} async-done(((bf16[256,128]{1,0:T(8,128)(2,1)}), bf16[16384,128]{1,0:T(8,128)(2,1)}) %all-gather.2.cloned.1.call-update) | async-done | bytes 4194320 | tf_op jit(solution)/shard_map/all_gather | solution.py:46
  154.8 2.9 gather_fusion
  157.7 1.9 fusion.7
  159.6 2.0 copy.15
  163.3 1.1 fusion.18
  164.5 1.1 fusion.17
  165.6 96.7 %psum.23 = f32[1024]{0:T(1024)S(1)} all-reduce(f32[1024]{0:T(1024)S(1)} %get-tuple-element.5), channel_id=1, replica_groups=mesh['dp'=8,'feat'=64] {'dp','feat'}, use_global_device_ids=true, to_apply=%region_3.0 | all-reduce | flops 1024 | bytes 8192 | tf_op jit(solution)/shard_map/psum | solution.py:65
  262.9 174.5 %all-reduce.3.cloned.1.call-done = (f32[128,1024]{0,1:T(8,128)}, f32[128,1024]{0,1:T(8,128)}) async-done(((f32[128,1024]{0,1:T(8,128)}, f32[128,1024]{0,1:T(8,128)}), (f32[128,1024]{0,1:T(8,128)}, f32[128,1024]{0,1:T(8,128)})) %all-reduce.3.cloned.1.call-update) | async-done | bytes 1048592 | tf_op jit(solution)/shard_map/psum | solution.py:65
  437.4 1.3 constant_dynamic-slice_fusion
  (74 shorter events, 38.9 us)
Async XLA Ops:
  7.2 150.6 %copy-start = (bf16[1,24,128,128]{3,2,1,0:T(8,128)(2,1)S(1)}, bf16[1,24,128,128]{3,2,1,0:T(8,128)(2,1)}, u32[]{:S(2)}) copy-start(bf16[1,24,128,128]{3,2,1,0:T(8,128)(2,1)} %param.11) | copy-start | bytes 2359300
  7.2 147.7 %all-gather.2.cloned.1.call-start = ((), (), s32[]{:S(2)}) async-start(), calls=%async_computation.1 | async-start | bytes 4259840 | tf_op jit(solution)/shard_map/all_gather | solution.py:46
  74.0 363.5 %all-reduce.3.cloned.1.call-start = ((), (), s32[]{:S(2)}) async-start(), calls=%async_computation.2 | async-start | bytes 2097152 | tf_op jit(solution)/shard_map/psum | solution.py:65
  159.6 2.0 copy-start.1
  161.6 1.0 copy-start.2
  161.6 1.1 copy-start.3
  161.6 1.1 copy-start.4
Sparse Core Ops, SparseCore 0:
  74.1 80.7 all-gather.1
  165.8 271.6 all-reduce.2
